TPU v7x, 128 devices: a whole 4x4x4 slice. The times are simulated.
128 devices in a mesh: node: 32 (over z, y, core), pb: 4 (over x).
Axes of the slice: x: 4, y: 4, z: 4, core: 2. Of those that a mesh axis runs over, the one named last changes fastest.
Arguments:
- node_scores: bfloat16 [262144, 512], P('node', 'pb'), may hold values from -8 to 8
- seeds: int32 [512], P('pb'), may hold values from 0 to 262143
- node_lists: int32 [2048, 8], P('node'), may hold values from 0 to 127
- node_tiles: bfloat16 [2048, 8, 128, 128], P('node'), as said below
- anchor_lists: int32 [128, 4], replicated, may hold values from 0 to 127
- anchor_tiles: bfloat16 [128, 4, 128, 128], P('node'), as said below
Outputs:
- ranking: bfloat16 [262144, 512], P('node', 'pb')
- anchor_scores: float32 [16384, 512], P('node', 'pb')
Inputs may be any that keep to these rules, and one draw needn't show every extreme that they name: `node_tiles`: entries of order 1 / sqrt(16384). `anchor_tiles`: entries of order 0.5 / sqrt(512).
All inputs are finite; a program needn't handle non-finite values.
Results may differ from a plain program's by a relative error of at most 0.011.
Values may be sent and summed in bfloat16 or wider, within the bound.
A program may use at most 192 MiB of HBM per device.

v0:
```python
import jax
import jax.numpy as jnp
from jax import lax
from jax.sharding import PartitionSpec as P

ITERS = 2


SEED_GAIN = 4.0
EPS = 1e-05


def share_values(values):
    return lax.all_gather(values.astype(jnp.bfloat16), "node", axis=0, tiled=True)


def shards(node_scores, seeds, node_lists, node_tiles, anchor_lists, anchor_tiles):
    blocks_dev, links, width, _ = node_tiles.shape
    rows_dev, columns = node_scores.shape
    owned = anchor_tiles.shape[0]
    start_row = lax.axis_index("node") * rows_dev
    rows = start_row + jnp.arange(rows_dev, dtype=jnp.int32)
    hit = (rows[:, None] == seeds[None, :]).astype(jnp.float32)
    seeded = (node_scores.astype(jnp.float32) + SEED_GAIN * hit).astype(jnp.bfloat16)
    blocks = seeded.reshape(blocks_dev, width, columns)
    terms = jnp.einsum("bkij,biq->bkjq", node_tiles, blocks, preferred_element_type=jnp.float32)
    flat_terms = terms.reshape(blocks_dev * links, width * columns)
    flat_ids = node_lists.reshape(-1)
    count = lax.axis_size("node") * (owned * width)
    span = count // width
    local = flat_ids
    valid = (local >= 0) & (local < span)
    local = jnp.where(valid, local, span)
    held = jnp.zeros((span, width * columns), jnp.float32).at[local].add(flat_terms, mode="drop")
    sums = lax.psum_scatter(
        held.reshape(count, columns), "node", scatter_dimension=0, tiled=True
    ).reshape(owned, width, columns)
    own_lists = lax.dynamic_slice_in_dim(anchor_lists, lax.axis_index("node") * owned, owned, 0)
    values = sums
    for step in range(ITERS):
        current = share_values(values)
        near = current[own_lists]
        values = sums + jnp.einsum(
            "akij,akjq->aiq", anchor_tiles, near, preferred_element_type=jnp.float32
        )
    final_shared = share_values(values)
    anchor_scores = values.reshape(owned * width, columns)
    picked = final_shared[node_lists]
    back = jnp.einsum("bkij,bkjq->biq", node_tiles, picked, preferred_element_type=jnp.float32)
    resid = seeded.astype(jnp.float32) - back.reshape(rows_dev, columns)
    energy = lax.psum(jnp.sum(resid * resid, axis=1).astype(jnp.bfloat16), "pb").astype(jnp.float32)
    total_columns = columns * lax.axis_size("pb")
    ranking = (resid * lax.rsqrt(energy / total_columns + EPS)[:, None]).astype(jnp.bfloat16)
    return (ranking, anchor_scores)


def solution(mesh):
    in_specs = (
        P("node", "pb"),
        P("pb"),
        P("node", None),
        P("node", None, None, None),
        P(),
        P("node", None, None, None),
    )
    out_specs = (P("node", "pb"), P("node", "pb"))
    return jax.shard_map(shards, mesh=mesh, in_specs=in_specs, out_specs=out_specs, check_vma=False)
```

profile of v0, /device:TPU:0, one launch (start us, length us, event | category | flops | bytes accessed | tf_op | source)
XLA Modules:
  0.0 535.9 jit_solution(2737357985444646289)
XLA Ops:
  7.2 0.8 copy.21
  8.0 0.1 reshape.71
  8.2 5.5 %add_convert_fusion = bf16[8192,128]{1,0:T(8,128)(2,1)S(1)} fusion(bf16[8192,128]{1,0:T(8,128)(2,1)} %param.6, s32[128]{0:T(128)} %param.7, s32[8192]{0:T(1024)S(1)} %iota_add_fusion), kind=kLoop, calls=%fused_computation.11 | loop fusion | flops 5242880 | bytes 4227584 | tf_op jit(solution)/shard_map/convert_element_type | solution.py:24
  13.7 21.4 %convolution_bitcast_fusion = f32[64,8,128,128]{2,3,1,0:T(8,128)} fusion(bf16[64,128,128,1]{2,1,3,0:T(8,128)(2,1)S(1)} %bitcast.55, bf16[64,8,128,128]{3,2,1,0:T(8,128)(2,1)} %param.9), kind=kOutput, calls=%fused_computation.5 | convolution fusion | flops 2147483648 | bytes 52428800 | tf_op jit(solution)/shard_map/bkij,biq->bkjq/dot_general | solution.py:26
  35.0 33.4 %copy.23 = f32[64,8,128,128]{3,2,1,0:T(8,128)} copy(f32[64,8,128,128]{2,3,1,0:T(8,128)} %convolution_bitcast_fusion) | data formatting | bytes 67108864 | tf_op jit(solution)/shard_map/bkij,biq->bkjq/dot_general | solution.py:26
  68.4 32.9 %copy.38 = f32[64,8,128,128]{3,1,2,0:T(8,128)} copy(f32[64,8,128,128]{3,2,1,0:T(8,128)} %copy.23) | data formatting | bytes 67108864
  101.4 111.2 %scatter_custom_fusion = f32[128,16384]{1,0:T(8,128)} fusion(s32[512]{0:T(512)S(1)} %bitcast.62, f32[512,16384]{1,0:T(8,128)} %bitcast.54, f32[]{:T(128)} %constant.14.clone.1), kind=kCustom, calls=%fused_computation.9 | custom fusion | flops 8388608 | bytes 8389120 | tf_op jit(solution)/shard_map/scatter-add | solution.py:34
  212.6 9.2 %reshape.74 = f32[16384,128]{1,0:T(8,128)} reshape(f32[128,16384]{1,0:T(8,128)} %scatter_custom_fusion) | data formatting | bytes 16777216 | tf_op jit(solution)/shard_map/reshape | solution.py:36
  221.8 0.0 all-gather.4.cloned.1.call-start
  221.9 95.4 %reduce-scatter.2.cloned.1.call-done = f32[512,128]{1,0:T(8,128)} async-done(((f32[16384,128]{1,0:T(8,128)}), f32[512,128]{1,0:T(8,128)}) %reduce-scatter.2.cloned.1.call-update) | async-done | bytes 262160 | tf_op jit(solution)/shard_map/reduce_scatter | solution.py:35
  317.3 1.7 convert_element_type.31
  319.0 0.0 all-gather.6.cloned.1.call-start
  319.1 0.1 compare_select_fusion.2
  319.2 0.1 copy.24
  319.3 0.1 reshape.80
  319.4 1.1 copy.26
  320.5 45.6 %all-gather.4.cloned.1.call-done = bf16[128,128,128]{2,1,0:T(8,128)(2,1)} async-done(((bf16[4,128,128]{2,1,0:T(8,128)(2,1)}), bf16[128,128,128]{2,1,0:T(8,128)(2,1)}) %all-gather.4.cloned.1.call-update) | async-done | bytes 4194320 | tf_op jit(solution)/shard_map/all_gather | solution.py:14
  366.1 2.8 gather_fusion
  368.9 0.3 fusion.4
  369.3 0.8 copy.27
  370.0 0.0 all-gather.8.cloned.1.call-start
  370.1 45.8 %all-gather.6.cloned.1.call-done = bf16[128,128,128]{2,1,0:T(8,128)(2,1)} async-done(((bf16[4,128,128]{2,1,0:T(8,128)(2,1)}), bf16[128,128,128]{2,1,0:T(8,128)(2,1)}) %all-gather.6.cloned.1.call-update) | async-done | bytes 4194320 | tf_op jit(solution)/shard_map/all_gather | solution.py:14
  415.9 2.8 gather_fusion.1
  418.7 1.0 fusion.5
  419.8 0.1 copy.28
  419.9 0.1 reshape.96
  420.0 45.6 %all-gather.8.cloned.1.call-done = bf16[128,128,128]{2,1,0:T(8,128)(2,1)} async-done(((bf16[4,128,128]{2,1,0:T(8,128)(2,1)}), bf16[128,128,128]{2,1,0:T(8,128)(2,1)}) %all-gather.8.cloned.1.call-update) | async-done | bytes 4194320 | tf_op jit(solution)/shard_map/all_gather | solution.py:14
  465.6 16.1 %gather_fusion.2 = bf16[512,128,128]{2,1,0:T(8,128)(2,1)} fusion(bf16[128,128,128]{2,1,0:T(8,128)(2,1)} %all-gather.8.cloned.1.call-done, s32[1024]{0:T(1024)S(1)} %pad_clamp_fusion), kind=kCustom, calls=%fused_computation.2 | custom fusion | bytes 33556480 | tf_op jit(solution)/shard_map/gather | solution.py:48
  481.7 17.2 %fusion.6 = f32[64,128,128,1]{1,2,3,0:T(8,128)} fusion(bf16[64,8,128,128]{3,2,1,0:T(8,128)(2,1)} %param.9, bf16[64,8,128,128]{3,2,1,0:T(8,128)(2,1)} %bitcast.53), kind=kOutput, calls=%fused_computation.26 | convolution fusion | flops 2147483648 | bytes 37748736 | tf_op jit(solution)/shard_map/bkij,bkjq->biq/dot_general | solution.py:49
  498.9 4.4 multiply_reduce_fusion
  503.3 16.8 %psum.7 = bf16[8192]{0:T(1024)(128)(2,1)S(1)} all-reduce(bf16[8192]{0:T(1024)(128)(2,1)S(1)} %multiply_reduce_fusion), channel_id=1, replica_groups=mesh['node'=32,'pb'=4] {'pb'}, use_global_device_ids=true, to_apply=%region_3.4 | all-reduce | flops 8192 | bytes 32768 | tf_op jit(solution)/shard_map/psum | solution.py:51
  520.2 8.9 %multiply_convert_fusion = bf16[8192,128]{1,0:T(8,128)(2,1)} fusion(f32[64,128,128,1]{1,2,3,0:T(8,128)} %fusion.6, f32[8192]{0:T(1024)S(1)} %add_rsqrt_fusion, s32[128]{0:T(128)S(1)} %copy-done.4, s32[8192]{0:T(1024)S(1)} %iota_add_fusion, bf16[8192,128]{1,0:T(8,128)(2,1)S(1)} %copy-done.1), kind=kLoop, calls=%fused_computation.7 | loop fusion | flops 9437184 | bytes 8454656 | tf_op jit(solution)/shard_map/convert_element_type | solution.py:53
  (23 shorter events, 0.2 us)
Async XLA Ops:
  7.2 361.7 %copy-start = (bf16[4,4,128,128]{3,2,1,0:T(8,128)(2,1)S(1)}, bf16[4,4,128,128]{3,2,1,0:T(8,128)(2,1)}, u32[]{:S(2)}) copy-start(bf16[4,4,128,128]{3,2,1,0:T(8,128)(2,1)} %param.11) | copy-start | bytes 1572868
  7.2 310.1 %reduce-scatter.2.cloned.1.call-start = ((), (), s32[]{:S(2)}) async-start(), calls=%async_computation.1 | async-start | bytes 8650752 | tf_op jit(solution)/shard_map/reduce_scatter | solution.py:35
  221.8 97.3 %copy-start.5 = (s32[128,4]{0,1:T(4,128)S(1)}, s32[128,4]{0,1:T(4,128)}, u32[]{:S(2)}) copy-start(s32[128,4]{0,1:T(4,128)} %param.10) | copy-start | bytes 6148
  221.8 198.0 %copy-start.3 = (s32[64,8]{0,1:T(8,128)S(1)}, s32[64,8]{0,1:T(8,128)}, u32[]{:S(2)}) copy-start(s32[64,8]{0,1:T(8,128)} %param.8) | copy-start | bytes 6148
  221.8 144.2 %all-gather.4.cloned.1.call-start = ((), (), s32[]{:S(2)}) async-start(), calls=%async_computation.2 | async-start | bytes 4325376 | tf_op jit(solution)/shard_map/all_gather | solution.py:14
  317.3 101.4 %copy-start.2 = (f32[512,128]{1,0:T(8,128)S(1)}, f32[512,128]{1,0:T(8,128)}, u32[]{:S(2)}) copy-start(f32[512,128]{1,0:T(8,128)} %reduce-scatter.2.cloned.1.call-done) | copy-start | bytes 786436
  319.0 96.8 %all-gather.6.cloned.1.call-start = ((), (), s32[]{:S(2)}) async-start(), calls=%async_computation.3 | async-start | bytes 4325376 | tf_op jit(solution)/shard_map/all_gather | solution.py:14
  370.0 95.6 %all-gather.8.cloned.1.call-start = ((), (), s32[]{:S(2)}) async-start(), calls=%async_computation.4 | async-start | bytes 4325376 | tf_op jit(solution)/shard_map/all_gather | solution.py:14
  481.7 17.2 %copy-start.1 = (bf16[8192,128]{1,0:T(8,128)(2,1)S(1)}, bf16[8192,128]{1,0:T(8,128)(2,1)}, u32[]{:S(2)}) copy-start(bf16[8192,128]{1,0:T(8,128)(2,1)} %param.6) | copy-start | bytes 6291460
  481.7 17.2 %copy-start.4 = (s32[128]{0:T(128)S(1)}, s32[128]{0:T(128)}, u32[]{:S(2)}) copy-start(s32[128]{0:T(128)} %param.7) | copy-start | bytes 1540
Sparse Core Ops, SparseCore 0:
  222.0 95.3 reduce-scatter.1
  320.4 45.5 all-gather.3
  370.2 45.6 all-gather.5
  419.9 45.6 all-gather.7
where the time goes:
time: 545 us; the launch traced here: 536 us
  waiting for transfers between devices  233 us (43%)
  other arithmetic  132 us (24%)
  local copies, waits for them, and re-layouts  101 us (19%)
  matrix products  39.9 us (7%)
  blocking collectives  16.8 us (3%)
  between operations  14.1 us (3%)
    all_gather x3, waiting for transfers between devices, share_values(): lax.all_gather(values.astype(jnp.bfloat16), 'node', axis=0, tiled=True)  137 us
    scatter-add x1, other arithmetic, shards(): jnp.zeros((span, width * columns), jnp.float32).at[local]  111 us
    reduce_scatter x1, waiting for transfers between devices, shards(): lax.psum_scatter(held.reshape(count, columns), 'node', scatter_dimension=...  95.4 us
    unnamed x14, local copies, waits for them, and re-layouts  33.8 us
    dot_general x1, local copies, waits for them, and re-layouts, shards(): jnp.einsum('bkij,biq->bkjq', node_tiles, blocks, preferred_element_type=j...  33.4 us
    dot_general x1, matrix products, shards(): jnp.einsum('bkij,biq->bkjq', node_tiles, blocks, preferred_element_type=j...  21.4 us
    dot_general x1, matrix products, shards(): jnp.einsum('bkij,bkjq->biq', node_tiles, picked, preferred_element_type=j...  17.2 us
    psum x1, blocking collectives, shards(): lax.psum(jnp.sum(resid * resid, axis=1).astype(jnp.bfloat16), 'pb')  16.8 us
  transfers between devices with their start and end apart: 4, of which 4 were waited for; matrix products, arithmetic and copies ran while one was open for 0% of the time, Pallas kernels for 0%

commit v1 on v0

v1 whole, which is shorter than its diff:
```python
import functools

import jax
import jax.numpy as jnp
from jax import lax
from jax.experimental import pallas as pl
from jax.experimental.pallas import tpu as pltpu
from jax.sharding import PartitionSpec as P

ITERS = 2
SEED_GAIN = 4.0
EPS = 1e-05
B = 128
NB = 64
KN = 8
KA = 4
NA = 128
H = 2
R = B // H
STEP = 8
F32 = jnp.float32
BF16 = jnp.bfloat16
MESH = pl.DeviceIdType.MESH


def place(ids):
    z, y, core, slot = ids // 32, (ids // 8) % 4, (ids // 4) % 2, ids % 4
    first = z + core * (y - z)
    second = y + core * (z - y)
    return core * 64 + first * 16 + second * 4 + slot


def forward_kernel(places, seeds, scores, tiles, held, seeded, total):
    step = pl.program_id(0)
    start_row = lax.axis_index("node") * (NB * B)

    @pl.when(step == 0)
    def _():
        def clear(i, carry):
            total[i] = jnp.zeros((B, B), F32)
            return carry

        lax.fori_loop(0, NA, clear, 0, unroll=4)

    wanted = seeds[...]
    for b in range(STEP):
        first = start_row + (step * STEP + b) * B
        rows = lax.broadcasted_iota(jnp.int32, (B, B), 0) + first
        hit = (rows == wanted).astype(F32)
        block = scores[b * B : (b + 1) * B, :].astype(F32) + SEED_GAIN * hit
        flipped = block.T.astype(BF16)
        seeded[b] = flipped
        for k in range(KN):
            term = jnp.dot(flipped, tiles[b, k], preferred_element_type=F32)
            at = places[(step * STEP + b) * KN + k]
            total[at] += term

    @pl.when(step == pl.num_programs(0) - 1)
    def _():
        def narrow(i, carry):
            whole = total[i].astype(BF16)
            for h in range(H):
                held[h, i] = whole[h * R : (h + 1) * R]
            return carry

        lax.fori_loop(0, NA, narrow, 0, unroll=4)


def forward(places, seeds, scores, tiles):
    return pl.pallas_call(
        forward_kernel,
        grid_spec=pltpu.PrefetchScalarGridSpec(
            num_scalar_prefetch=1,
            grid=(NB // STEP,),
            in_specs=[
                pl.BlockSpec((1, B), lambda g, p: (0, 0)),
                pl.BlockSpec((STEP * B, B), lambda g, p: (g, 0)),
                pl.BlockSpec((STEP, KN, B, B), lambda g, p: (g, 0, 0, 0)),
            ],
            out_specs=[
                pl.BlockSpec((H, NA, R, B), lambda g, p: (0, 0, 0, 0)),
                pl.BlockSpec((STEP, B, B), lambda g, p: (g, 0, 0)),
            ],
            scratch_shapes=[pltpu.VMEM((NA, B, B), F32)],
        ),
        out_shape=[
            jax.ShapeDtypeStruct((H, NA, R, B), BF16),
            jax.ShapeDtypeStruct((NB, B, B), BF16),
        ],
        compiler_params=pltpu.CompilerParams(vmem_limit_bytes=40 << 20),
        cost_estimate=pl.CostEstimate(flops=2 * NB * KN * B**3, bytes_accessed=24 << 20, transcendentals=0),
        name="forward",
    )(places, seeds, scores, tiles)


CHUNKS = 4
PER = NB // CHUNKS
RS_SEMS = 4 + 6 + 6
AG_SEMS = 4 + 6 + 4
HALF_SEMS = RS_SEMS + (ITERS + 1) * AG_SEMS


def rest_kernel(places, near, held, seeded_in, atiles, tiles_in, rank_out, score_out, *scratch):
    scratch = list(scratch)
    take = lambda n: [scratch.pop(0) for _ in range(n)]
    tiles, seeded, resid, energy, others, ranked = take(6)
    own, mate = take(H), take(H)
    far, up, down, ra, rb, gm, gp = (take(H) for _ in range(7))
    far2, up2, down2, ra2, rb2, gm2, gp2 = (take(H) for _ in range(7))
    sums, values = take(H), take(H)
    shared = [take(H) for _ in range(ITERS + 1)]
    send_sems, recv_sems, local_sems, esend, erecv = take(5)

    node, pb = lax.axis_index("node"), lax.axis_index("pb")
    core = node % 2
    sf, ss = 8 - 6 * core, 2 + 6 * core
    pf, ps = (node // sf) % 4, (node // ss) % 4
    turn = lambda at, by: (at + by + 4) % 4
    f_up = node + (turn(pf, 1) - pf) * sf
    f_dn = node + (turn(pf, -1) - pf) * sf
    s_up = node + (turn(ps, 1) - ps) * ss
    s_dn = node + (turn(ps, -1) - ps) * ss
    sib = node + 1 - 2 * core

    locals_ = []

    def local(src, dst):
        copy = pltpu.make_async_copy(src, dst, local_sems.at[len(locals_)])
        copy.start()
        locals_.append(copy)
        return copy

    own_copies = [local(held.at[h, pl.ds(core * 64, 64)], own[h]) for h in range(H)]
    seeded_copy = local(seeded_in, seeded)
    tile_copies = [local(tiles_in.at[pl.ds(i * PER, PER)], tiles.at[pl.ds(i * PER, PER)]) for i in range(CHUNKS)]

    barrier = pltpu.get_barrier_semaphore()
    for peer in (sib, f_up, f_dn, s_up, s_dn):
        pl.semaphore_signal(barrier, inc=1, device_id={"node": peer}, device_id_type=MESH)
    for by in (1, 2, 3):
        pl.semaphore_signal(barrier, inc=1, device_id={"pb": turn(pb, by)}, device_id_type=MESH)
    pl.semaphore_wait(barrier, 8)

    started = []
    count = [0] * H

    def send(h, src, dst, peer):
        i = h * HALF_SEMS + count[h]
        count[h] += 1
        copy = pltpu.make_async_remote_copy(
            src_ref=src, dst_ref=dst, send_sem=send_sems.at[i], recv_sem=recv_sems.at[i],
            device_id={"node": peer}, device_id_type=MESH,
        )
        copy.start()
        started.append(copy)
        return copy

    def add_blocks(n, dst, dst_at, *terms):
        def body(i, carry):
            for u in range(2):
                j = i * 2 + u
                acc = terms[0][0][terms[0][1] + j].astype(F32)
                for ref, at in terms[1:]:
                    acc = acc + ref[at + j].astype(F32)
                dst[dst_at + j] = acc.astype(dst.dtype)
            return carry

        lax.fori_loop(0, n // 2, body, 0)

    def reduce_scatter(h):
        o, m = own[h], mate[h]
        other = (1 - core) * 64
        got = {}
        for by in (2, 1, 3, 0):
            f = turn(ps, by)
            got[by] = send(h, held.at[h, pl.ds(other + f * 16, 16)], m.at[pl.ds(f * 16, 16)], sib)
        yield
        own_copies[h].wait()
        got[2].wait_recv()
        at = turn(pf, 2) * 16
        add_blocks(16, far[h], 0, (o, at), (m, at))
        a1 = send(h, far[h].at[pl.ds(0, 8)], ra[h], f_up)
        b1 = send(h, far[h].at[pl.ds(8, 8)], rb[h], f_dn)
        at_up, at_dn = turn(pf, 1) * 16, turn(pf, -1) * 16
        got[1].wait_recv()
        add_blocks(8, up[h], 8, (o, at_up + 8), (m, at_up + 8))
        mb = send(h, up[h].at[pl.ds(8, 8)], gm[h].at[pl.ds(8, 8)], f_up)
        got[3].wait_recv()
        add_blocks(8, down[h], 0, (o, at_dn), (m, at_dn))
        pa = send(h, down[h].at[pl.ds(0, 8)], gp[h].at[pl.ds(0, 8)], f_dn)
        yield
        a1.wait_recv()
        add_blocks(8, up[h], 0, (o, at_up), (m, at_up), (ra[h], 0))
        ma = send(h, up[h].at[pl.ds(0, 8)], gm[h].at[pl.ds(0, 8)], f_up)
        b1.wait_recv()
        add_blocks(8, down[h], 8, (o, at_dn + 8), (m, at_dn + 8), (rb[h], 0))
        pb_ = send(h, down[h].at[pl.ds(8, 8)], gp[h].at[pl.ds(8, 8)], f_dn)
        yield
        got[0].wait_recv()
        for copy in (mb, pa, ma, pb_):
            copy.wait_recv()
        mine = pf * 16

        def part(s, skip):
            at = s * 4 + skip
            return (o, mine + at), (m, mine + at), (gm[h], at), (gp[h], at)

        s_far, s_a, s_b = turn(ps, 2), turn(ps, 1), turn(ps, -1)
        add_blocks(4, far2[h], 0, *part(s_far, 0))
        a1 = send(h, far2[h].at[pl.ds(0, 2)], ra2[h], s_up)
        b1 = send(h, far2[h].at[pl.ds(2, 2)], rb2[h], s_dn)
        add_blocks(2, up2[h], 2, *part(s_a, 2))
        mb = send(h, up2[h].at[pl.ds(2, 2)], gm2[h].at[pl.ds(2, 2)], s_up)
        add_blocks(2, down2[h], 0, *part(s_b, 0))
        pa = send(h, down2[h].at[pl.ds(0, 2)], gp2[h].at[pl.ds(0, 2)], s_dn)
        yield
        a1.wait_recv()
        add_blocks(2, up2[h], 0, *part(s_a, 0), (ra2[h], 0))
        ma = send(h, up2[h].at[pl.ds(0, 2)], gm2[h].at[pl.ds(0, 2)], s_up)
        b1.wait_recv()
        add_blocks(2, down2[h], 2, *part(s_b, 2), (rb2[h], 0))
        pb_ = send(h, down2[h].at[pl.ds(2, 2)], gp2[h].at[pl.ds(2, 2)], s_dn)
        yield
        for copy in (mb, pa, ma, pb_):
            copy.wait_recv()
        add_blocks(4, sums[h], 0, *part(ps, 0), (gm2[h], 0), (gp2[h], 0))

    def all_gather(h, buf):
        row = core * 64 + pf * 16
        mine = row + ps * 4
        at = lambda start, n: buf.at[pl.ds(start, n)]
        go = lambda start, n, peer: send(h, at(start, n), at(start, n), peer)
        u1 = go(mine, 4, s_up)
        d1 = go(mine, 4, s_dn)
        yield
        u1.wait_recv()
        u2 = go(row + turn(ps, -1) * 4, 2, s_up)
        d1.wait_recv()
        d2 = go(row + turn(ps, 1) * 4 + 2, 2, s_dn)
        yield
        u2.wait_recv()
        d2.wait_recv()
        ua = go(row, 8, f_up)
        db = go(row + 8, 8, f_dn)
        ub = go(row + 8, 8, f_up)
        da = go(row, 8, f_dn)
        across = [go(row, 16, sib)]
        yield
        base = core * 64
        low, high, far_ = base + turn(pf, -1) * 16, base + turn(pf, 1) * 16, base + turn(pf, 2) * 16
        ua.wait_recv()
        ua2 = go(low, 8, f_up)
        db.wait_recv()
        db2 = go(high + 8, 8, f_dn)
        yield
        ub.wait_recv()
        across.append(go(low, 16, sib))
        da.wait_recv()
        across.append(go(high, 16, sib))
        yield
        ua2.wait_recv()
        db2.wait_recv()
        across.append(go(far_, 16, sib))
        yield
        for copy in across:
            copy.wait_recv()

    def iterate(h, buf, out, keep):
        mine = core * 64 + pf * 16 + ps * 4
        for r in range(4):
            acc = sums[h][r]
            for k in range(0, KA, 2):
                left = jnp.concatenate([buf[near[r * KA + k + i]] for i in range(2)], axis=1)
                right = jnp.concatenate([atiles[r, k + i] for i in range(2)], axis=1)
                acc = acc + lax.dot_general(left, right, (((1,), (1,)), ((), ())), preferred_element_type=F32)
            if keep is not None:
                keep[r] = acc
            out[mine + r] = acc.astype(BF16)

    def pipeline(h):
        yield from reduce_scatter(h)
        mine = core * 64 + pf * 16 + ps * 4
        for r in range(4):
            shared[0][h][mine + r] = sums[h][r].astype(BF16)
        for t in range(ITERS):
            yield from all_gather(h, shared[t][h])
            iterate(h, shared[t][h], shared[t + 1][h], values[h] if t == ITERS - 1 else None)
        yield from all_gather(h, shared[ITERS][h])

    lines = [pipeline(h) for h in range(H)]
    live = list(range(H))
    next(lines[0])
    if H > 1:
        next(lines[1])
    while live:
        for h in list(live):
            try:
                next(lines[h])
            except StopIteration:
                live.remove(h)

    for r in range(4):
        whole = jnp.concatenate([values[h][r] for h in range(H)], axis=0)
        score_out[r * B : (r + 1) * B, :] = whole.T

    seeded_copy.wait()
    final = shared[ITERS]
    esends = []
    outs = []

    def finish(c):
        for copy in esends[c]:
            copy.wait_recv()

        def body(i, carry):
            for u in range(2):
                b = c * PER + i * 2 + u
                tot = energy[pl.ds(b, 1), :]
                for d in range(3):
                    tot = tot + others[d, pl.ds(b, 1), :]
                scale = lax.rsqrt(tot / 512.0 + EPS)
                block = (resid[b] * scale).astype(BF16)
                ranked[pl.ds(pl.multiple_of(b * B, B), B), :] = block.T
            return carry

        lax.fori_loop(0, PER // 2, body, 0)
        copy = pltpu.make_async_copy(
            ranked.at[pl.ds(c * PER * B, PER * B)], rank_out.at[pl.ds(c * PER * B, PER * B)],
            local_sems.at[H + 1 + CHUNKS + c],
        )
        copy.start()
        outs.append(copy)

    for c in range(CHUNKS):
        tile_copies[c].wait()

        def body(i, carry):
            for u in range(4):
                b = c * PER + i * 4 + u
                acc = None
                for k in range(0, KN, 2):
                    pieces = []
                    for j in range(2):
                        at = places[b * KN + k + j]
                        pieces.append(jnp.concatenate([final[h][at] for h in range(H)], axis=0))
                    left = jnp.concatenate(pieces, axis=1)
                    right = jnp.concatenate([tiles[b, k + j] for j in range(2)], axis=1)
                    part = lax.dot_general(left, right, (((1,), (1,)), ((), ())), preferred_element_type=F32)
                    acc = part if acc is None else acc + part
                res = seeded[b].astype(F32) - acc
                resid[b] = res
                energy[pl.ds(b, 1), :] = jnp.sum(res * res, axis=0, keepdims=True)
            return carry

        lax.fori_loop(0, PER // 4, body, 0)
        group = []
        for d in (1, 2, 3):
            i = c * 3 + d - 1
            copy = pltpu.make_async_remote_copy(
                src_ref=energy.at[pl.ds(c * PER, PER)], dst_ref=others.at[d - 1, pl.ds(c * PER, PER)],
                send_sem=esend.at[i], recv_sem=erecv.at[i],
                device_id={"pb": turn(pb, d)}, device_id_type=MESH,
            )
            copy.start()
            group.append(copy)
        esends.append(group)
        if c > 0:
            finish(c - 1)
    finish(CHUNKS - 1)

    for copy in started:
        copy.wait_send()
    for group in esends:
        for copy in group:
            copy.wait_send()
    for copy in outs:
        copy.wait()


def rest(places, near, held, seeded, atiles, tiles):
    vm = lambda *shape, dtype=BF16: pltpu.VMEM(shape, dtype)
    per_half = lambda n, dtype=BF16: [pltpu.VMEM((n, R, B), dtype) for _ in range(H)]
    scratch = [
        vm(NB, KN, B, B),
        vm(NB, B, B),
        vm(NB, B, B, dtype=F32),
        vm(NB, B, dtype=F32),
        vm(3, NB, B, dtype=F32),
        vm(NB * B, B),
    ]
    for n in (64, 64, 16, 16, 16, 8, 8, 16, 16, 4, 4, 4, 2, 2, 4, 4):
        scratch += per_half(n)
    scratch += per_half(4, F32) + per_half(4, F32)
    for _ in range(ITERS + 1):
        scratch += per_half(NA)
    sems = pltpu.SemaphoreType.DMA
    scratch += [
        sems((H * HALF_SEMS,)), sems((H * HALF_SEMS,)), sems((H + 1 + 2 * CHUNKS,)),
        sems((3 * CHUNKS,)), sems((3 * CHUNKS,)),
    ]
    smem = pl.BlockSpec(memory_space=pltpu.SMEM)
    vmem = pl.BlockSpec(memory_space=pltpu.VMEM)
    hbm = pl.BlockSpec(memory_space=pl.ANY)
    return pl.pallas_call(
        rest_kernel,
        in_specs=[smem, smem, hbm, hbm, vmem, hbm],
        out_specs=[hbm, vmem],
        out_shape=[jax.ShapeDtypeStruct((NB * B, B), BF16), jax.ShapeDtypeStruct((4 * B, B), F32)],
        scratch_shapes=scratch,
        compiler_params=pltpu.CompilerParams(
            collective_id=0, has_side_effects=True, vmem_limit_bytes=58 << 20
        ),
        cost_estimate=pl.CostEstimate(flops=2 * NB * KN * B**3, bytes_accessed=28 << 20, transcendentals=0),
        name="rest",
    )(places, near, held, seeded, atiles, tiles)


def shards(node_scores, seeds, node_lists, node_tiles, anchor_lists, anchor_tiles):
    places = place(node_lists).reshape(-1)
    own_lists = lax.dynamic_slice_in_dim(anchor_lists, lax.axis_index("node") * 4, 4, 0)
    near = place(own_lists).reshape(-1)
    held, seeded = forward(places, seeds.reshape(1, B), node_scores, node_tiles)
    ranking, anchor_scores = rest(places, near, held, seeded, anchor_tiles, node_tiles)
    return (ranking, anchor_scores)


def solution(mesh):
    in_specs = (
        P("node", "pb"),
        P("pb"),
        P("node", None),
        P("node", None, None, None),
        P(),
        P("node", None, None, None),
    )
    out_specs = (P("node", "pb"), P("node", "pb"))
    return jax.shard_map(shards, mesh=mesh, in_specs=in_specs, out_specs=out_specs, check_vma=False)
```

time: 545 us -> 128 us (0.23); the launches traced: 536 us -> 127 us
  waiting for transfers between devices: 233 us -> 0 us
  other arithmetic: 132 us -> 1.49 us
  Pallas kernels: 0 us -> 114 us
  local copies, waits for them, and re-layouts: 101 us -> 10.2 us
  matrix products: 39.9 us -> 0 us
  blocking collectives: 16.8 us -> 0 us
  between operations: 14.1 us -> 0.69 us
    all_gather x3 -> x0, waiting for transfers between devices: 137 us -> none  [share_values(): lax.all_gather(values.astype(jnp.bfloat16), 'node', axis=0, tiled=True)]
    pallas_call x0 -> x2, Pallas kernels: none -> 114 us  [the longest x1 102 us: rest(): pl.pallas_call(rest_kernel, in_specs=[smem, smem, hbm, hbm, vmem, hbm], o...]
    scatter-add x1 -> x0, other arithmetic: 111 us -> none  [shards(): jnp.zeros((span, width * columns), jnp.float32).at[local]]
    reduce_scatter x1 -> x0, waiting for transfers between devices: 95.4 us -> none  [shards(): lax.psum_scatter(held.reshape(count, columns), 'node', scatter_dimension=...]
    dot_general x4 -> x0, matrix products: 39.9 us -> none  [the longest x1 21.4 us: shards(): jnp.einsum('bkij,biq->bkjq', node_tiles, blocks, preferred_element_type=j...]
    dot_general x1 -> x0, local copies, waits for them, and re-layouts: 33.4 us -> none  [shards(): jnp.einsum('bkij,biq->bkjq', node_tiles, blocks, preferred_element_type=j...]
    unnamed x14, local copies, waits for them, and re-layouts: 33.8 us -> 9.29 us
    gather x3 -> x0, local copies, waits for them, and re-layouts: 21.8 us -> none  [the longest x1 16.1 us: shards(): picked = final_shared[node_lists]]
  transfers between devices with their start and end apart: 4 -> 0, of which waited for: 4 -> 0; matrix products, arithmetic and copies ran while one was open for 0% -> 0% of each run, Pallas kernels for 0% -> 0%
where the time goes in v1:
time: 128 us; the launch traced here: 127 us
  Pallas kernels  114 us (89%)
  local copies, waits for them, and re-layouts  10.2 us (8%)
  other arithmetic  1.49 us (1%)
    pallas_call x1, Pallas kernels, rest(): pl.pallas_call(rest_kernel, in_specs=[smem, smem, hbm, hbm, vmem, hbm], o...  102 us
    pallas_call x1, Pallas kernels, forward(): pl.pallas_call(forward_kernel, grid_spec=pltpu.PrefetchScalarGridSpec(num...  12.7 us
    unnamed x14, local copies, waits for them, and re-layouts  9.29 us

profile of v1, /device:TPU:0, one launch (start us, length us, event | category | flops | bytes accessed | tf_op | source)
XLA Modules:
  0.0 126.8 jit_solution(13062044693382979778)
XLA Ops:
  0.6 0.8 fusion.14
  1.4 0.1 copy.10
  1.5 0.7 reshape.14.near
  2.2 0.7 fusion.4
  2.9 0.1 copy.9
  3.0 0.1 reshape.13.places
  3.1 0.0 copy-start.1
  3.1 1.6 %copy-done.1 = bf16[8192,128]{1,0:T(8,128)(2,1)S(1)} copy-done((bf16[8192,128]{1,0:T(8,128)(2,1)S(1)}, bf16[8192,128]{1,0:T(8,128)(2,1)}, u32[]{:S(2)}) %copy-start.1) | copy-done | bytes 2097176
  4.7 0.0 copy-start.4
  4.7 0.7 copy-done.4
  5.3 0.0 copy-start.3
  5.3 12.7 %forward.1 = (bf16[2,128,64,128]{3,2,1,0:T(8,128)(2,1)S(1)}, bf16[64,128,128]{2,1,0:T(8,128)(2,1)S(1)}) custom-call(s32[512]{0:T(512)S(1)} %reshape.13.places, s32[1,128]{1,0:T(1,128)S(1)} %bitcast.1, bf16[8192,128]{1,0:T(8,128)(2,1)S(1)} %copy-done.1, bf16[64,8,128,128]{3,2,1,0:T(8,128)(2,1)} %tiles_in.1), custom_call_target="tpu_custom_call" | custom-call | flops 2147483648 | bytes 25165824 | tf_op jit(solution)/shard_map/forward/pallas_call | solution.py:70
  18.0 0.0 copy-done.3
  18.0 0.0 copy-start
  18.0 1.9 %copy-done = bf16[2,128,64,128]{3,2,1,0:T(8,128)(2,1)} copy-done((bf16[2,128,64,128]{3,2,1,0:T(8,128)(2,1)}, bf16[2,128,64,128]{3,2,1,0:T(8,128)(2,1)S(1)}, u32[]{:S(2)}) %copy-start) | copy-done | bytes 4194328
  20.0 0.0 copy-start.2
  20.0 1.3 %copy-done.2 = bf16[64,128,128]{2,1,0:T(8,128)(2,1)} copy-done((bf16[64,128,128]{2,1,0:T(8,128)(2,1)}, bf16[64,128,128]{2,1,0:T(8,128)(2,1)S(1)}, u32[]{:S(2)}) %copy-start.2) | copy-done | bytes 2097176
  21.3 101.7 %rest.1 = (bf16[8192,128]{1,0:T(8,128)(2,1)}, f32[512,128]{1,0:T(8,128)}) custom-call(s32[512]{0:T(512)} %copy-done.3, s32[16]{0:T(128)} %reshape.14.near, bf16[2,128,64,128]{3,2,1,0:T(8,128)(2,1)} %copy-done, bf16[64,128,128]{2,1,0:T(8,128)(2,1)} %copy-done.2, bf16[4,4,128,128]{3,2,1,0:T(8,128)(2,1)} %atiles.1, bf16[64,8,128,128]{3,2,1,0:T(8,128)(2,1)} %tiles_in.1), custom_call_target="tpu_custom_call" | custom-call | flops 2147483648 | bytes 29360128 | tf_op jit(solution)/shard_map/rest/pallas_call | solution.py:404
  123.0 0.0 copy-start.5
  123.0 3.1 %copy.13 = bf16[8192,128]{1,0:T(8,128)(2,1)} copy(bf16[8192,128]{1,0:T(8,128)(2,1)} %get-tuple-element.8) | data formatting | bytes 4194304
  126.1 0.0 copy-done.5
  126.1 0.7 copy.14
Async XLA Ops:
  3.1 1.6 %copy-start.1 = (bf16[8192,128]{1,0:T(8,128)(2,1)S(1)}, bf16[8192,128]{1,0:T(8,128)(2,1)}, u32[]{:S(2)}) copy-start(bf16[8192,128]{1,0:T(8,128)(2,1)} %scores.1) | copy-start | bytes 6291460
  4.7 0.7 copy-start.4
  5.3 12.7 %copy-start.3 = (s32[512]{0:T(512)}, s32[512]{0:T(512)S(1)}, u32[]{:S(2)}) copy-start(s32[512]{0:T(512)S(1)} %reshape.13.places) | copy-start | bytes 6148
  18.0 1.9 %copy-start = (bf16[2,128,64,128]{3,2,1,0:T(8,128)(2,1)}, bf16[2,128,64,128]{3,2,1,0:T(8,128)(2,1)S(1)}, u32[]{:S(2)}) copy-start(bf16[2,128,64,128]{3,2,1,0:T(8,128)(2,1)S(1)} %get-tuple-element.4.held) | copy-start | bytes 12582916
  20.0 1.3 %copy-start.2 = (bf16[64,128,128]{2,1,0:T(8,128)(2,1)}, bf16[64,128,128]{2,1,0:T(8,128)(2,1)S(1)}, u32[]{:S(2)}) copy-start(bf16[64,128,128]{2,1,0:T(8,128)(2,1)S(1)} %get-tuple-element.5.seeded_in) | copy-start | bytes 6291460
  123.0 3.1 %copy-start.5 = (f32[512,128]{1,0:T(8,128)S(1)}, f32[512,128]{1,0:T(8,128)}, u32[]{:S(2)}) copy-start(f32[512,128]{1,0:T(8,128)} %get-tuple-element.9) | copy-start | bytes 786436

commit v2 on v1

--- a/solution.py
+++ b/solution.py
@@ -18,19 +18,20 @@
 H = 2
 R = B // H
 STEP = 8
+FORWARD_VMEM, REST_VMEM = 56, 50
 F32 = jnp.float32
 BF16 = jnp.bfloat16
 MESH = pl.DeviceIdType.MESH
 
 
 def place(ids):
-    z, y, core, slot = ids // 32, (ids // 8) % 4, (ids // 4) % 2, ids % 4
+    z, y, core, slot = ids >> 5, (ids >> 3) & 3, (ids >> 2) & 1, ids & 3
     first = z + core * (y - z)
     second = y + core * (z - y)
-    return core * 64 + first * 16 + second * 4 + slot
-
-
-def forward_kernel(places, seeds, scores, tiles, held, seeded, total):
+    return (core << 6) + (first << 4) + (second << 2) + slot
+
+
+def forward_kernel(lists, seeds, scores, tiles, held, seeded, total):
     step = pl.program_id(0)
     start_row = lax.axis_index("node") * (NB * B)
 
@@ -52,7 +53,7 @@
         seeded[b] = flipped
         for k in range(KN):
             term = jnp.dot(flipped, tiles[b, k], preferred_element_type=F32)
-            at = places[(step * STEP + b) * KN + k]
+            at = place(lists[k, step * STEP + b])
             total[at] += term
 
     @pl.when(step == pl.num_programs(0) - 1)
@@ -66,7 +67,7 @@
         lax.fori_loop(0, NA, narrow, 0, unroll=4)
 
 
-def forward(places, seeds, scores, tiles):
+def forward(lists, seeds, scores, tiles):
     return pl.pallas_call(
         forward_kernel,
         grid_spec=pltpu.PrefetchScalarGridSpec(
@@ -87,27 +88,29 @@
             jax.ShapeDtypeStruct((H, NA, R, B), BF16),
             jax.ShapeDtypeStruct((NB, B, B), BF16),
         ],
-        compiler_params=pltpu.CompilerParams(vmem_limit_bytes=40 << 20),
+        compiler_params=pltpu.CompilerParams(vmem_limit_bytes=FORWARD_VMEM << 20),
         cost_estimate=pl.CostEstimate(flops=2 * NB * KN * B**3, bytes_accessed=24 << 20, transcendentals=0),
         name="forward",
-    )(places, seeds, scores, tiles)
+    )(lists, seeds, scores, tiles)
 
 
 CHUNKS = 4
 PER = NB // CHUNKS
-RS_SEMS = 4 + 6 + 6
-AG_SEMS = 4 + 6 + 4
+RS_SEMS = 4 + 6 + 3
+AG_SEMS = 3 + 6 + 4
 HALF_SEMS = RS_SEMS + (ITERS + 1) * AG_SEMS
-
-
-def rest_kernel(places, near, held, seeded_in, atiles, tiles_in, rank_out, score_out, *scratch):
+TILE_SEMS = 3 * 4
+
+
+def rest_kernel(lists, near, held, seeded_in, atiles, tiles_in, rank_out, score_out, *scratch):
     scratch = list(scratch)
     take = lambda n: [scratch.pop(0) for _ in range(n)]
     tiles, seeded, resid, energy, others, ranked = take(6)
     own, mate = take(H), take(H)
     far, up, down, ra, rb, gm, gp = (take(H) for _ in range(7))
-    far2, up2, down2, ra2, rb2, gm2, gp2 = (take(H) for _ in range(7))
+    out2, in2 = take(H), take(H)
     sums, values = take(H), take(H)
+    (row_tiles,) = take(1)
     shared = [take(H) for _ in range(ITERS + 1)]
     send_sems, recv_sems, local_sems, esend, erecv = take(5)
 
@@ -120,6 +123,8 @@
     f_dn = node + (turn(pf, -1) - pf) * sf
     s_up = node + (turn(ps, 1) - ps) * ss
     s_dn = node + (turn(ps, -1) - ps) * ss
+    s_far = node + (turn(ps, 2) - ps) * ss
+    ring = ((2, s_far), (1, s_up), (-1, s_dn))
     sib = node + 1 - 2 * core
 
     locals_ = []
@@ -131,18 +136,19 @@
         return copy
 
     own_copies = [local(held.at[h, pl.ds(core * 64, 64)], own[h]) for h in range(H)]
+    own_tiles_copy = local(atiles, row_tiles.at[ps])
     seeded_copy = local(seeded_in, seeded)
     tile_copies = [local(tiles_in.at[pl.ds(i * PER, PER)], tiles.at[pl.ds(i * PER, PER)]) for i in range(CHUNKS)]
 
     barrier = pltpu.get_barrier_semaphore()
-    for peer in (sib, f_up, f_dn, s_up, s_dn):
+    for peer in (sib, f_up, f_dn, s_up, s_dn, s_far):
         pl.semaphore_signal(barrier, inc=1, device_id={"node": peer}, device_id_type=MESH)
     for by in (1, 2, 3):
         pl.semaphore_signal(barrier, inc=1, device_id={"pb": turn(pb, by)}, device_id_type=MESH)
-    pl.semaphore_wait(barrier, 8)
+    pl.semaphore_wait(barrier, 9)
 
     started = []
-    count = [0] * H
+    count = [0] * (H + 1)
 
     def send(h, src, dst, peer):
         i = h * HALF_SEMS + count[h]
@@ -154,6 +160,15 @@
         copy.start()
         started.append(copy)
         return copy
+
+    tile_sends = []
+
+    def share_tiles(n):
+        for _ in range(n):
+            i = len(tile_sends)
+            if i < 12:
+                r, (_, peer) = i // 3, ring[i % 3]
+                tile_sends.append(send(H, atiles.at[r], row_tiles.at[ps, r], peer))
 
     def add_blocks(n, dst, dst_at, *terms):
         def body(i, carry):
@@ -205,54 +220,42 @@
             at = s * 4 + skip
             return (o, mine + at), (m, mine + at), (gm[h], at), (gp[h], at)
 
-        s_far, s_a, s_b = turn(ps, 2), turn(ps, 1), turn(ps, -1)
-        add_blocks(4, far2[h], 0, *part(s_far, 0))
-        a1 = send(h, far2[h].at[pl.ds(0, 2)], ra2[h], s_up)
-        b1 = send(h, far2[h].at[pl.ds(2, 2)], rb2[h], s_dn)
-        add_blocks(2, up2[h], 2, *part(s_a, 2))
-        mb = send(h, up2[h].at[pl.ds(2, 2)], gm2[h].at[pl.ds(2, 2)], s_up)
-        add_blocks(2, down2[h], 0, *part(s_b, 0))
-        pa = send(h, down2[h].at[pl.ds(0, 2)], gp2[h].at[pl.ds(0, 2)], s_dn)
-        yield
-        a1.wait_recv()
-        add_blocks(2, up2[h], 0, *part(s_a, 0), (ra2[h], 0))
-        ma = send(h, up2[h].at[pl.ds(0, 2)], gm2[h].at[pl.ds(0, 2)], s_up)
-        b1.wait_recv()
-        add_blocks(2, down2[h], 2, *part(s_b, 2), (rb2[h], 0))
-        pb_ = send(h, down2[h].at[pl.ds(2, 2)], gp2[h].at[pl.ds(2, 2)], s_dn)
-        yield
-        for copy in (mb, pa, ma, pb_):
+        hops = []
+        for by, peer in ring:
+            to = turn(ps, by) * 4
+            add_blocks(4, out2[h], to, *part(turn(ps, by), 0))
+            hops.append(send(h, out2[h].at[pl.ds(to, 4)], in2[h].at[ps], peer))
+        share_tiles(3)
+        yield
+        add_blocks(4, sums[h], ps * 4, *part(ps, 0))
+        for copy in hops:
             copy.wait_recv()
-        add_blocks(4, sums[h], 0, *part(ps, 0), (gm2[h], 0), (gp2[h], 0))
-
-    def all_gather(h, buf):
-        row = core * 64 + pf * 16
+        for by in (2, 1, 3):
+            add_blocks(4, sums[h], ps * 4, (sums[h], ps * 4), (in2[h].at[turn(ps, by)], 0))
+
+    def all_gather(h, buf, whole):
+        base = core * 64
+        row = base + pf * 16
         mine = row + ps * 4
         at = lambda start, n: buf.at[pl.ds(start, n)]
         go = lambda start, n, peer: send(h, at(start, n), at(start, n), peer)
-        u1 = go(mine, 4, s_up)
-        d1 = go(mine, 4, s_dn)
-        yield
-        u1.wait_recv()
-        u2 = go(row + turn(ps, -1) * 4, 2, s_up)
-        d1.wait_recv()
-        d2 = go(row + turn(ps, 1) * 4 + 2, 2, s_dn)
-        yield
-        u2.wait_recv()
-        d2.wait_recv()
+        if not whole:
+            hops = [go(mine, 4, peer) for _, peer in ring]
+            share_tiles(3)
+            yield
+            for copy in hops:
+                copy.wait_recv()
         ua = go(row, 8, f_up)
         db = go(row + 8, 8, f_dn)
         ub = go(row + 8, 8, f_up)
         da = go(row, 8, f_dn)
         across = [go(row, 16, sib)]
         yield
-        base = core * 64
         low, high, far_ = base + turn(pf, -1) * 16, base + turn(pf, 1) * 16, base + turn(pf, 2) * 16
         ua.wait_recv()
         ua2 = go(low, 8, f_up)
         db.wait_recv()
         db2 = go(high + 8, 8, f_dn)
-        yield
         ub.wait_recv()
         across.append(go(low, 16, sib))
         da.wait_recv()
@@ -265,27 +268,38 @@
         for copy in across:
             copy.wait_recv()
 
-    def iterate(h, buf, out, keep):
-        mine = core * 64 + pf * 16 + ps * 4
-        for r in range(4):
-            acc = sums[h][r]
-            for k in range(0, KA, 2):
-                left = jnp.concatenate([buf[near[r * KA + k + i]] for i in range(2)], axis=1)
-                right = jnp.concatenate([atiles[r, k + i] for i in range(2)], axis=1)
-                acc = acc + lax.dot_general(left, right, (((1,), (1,)), ((), ())), preferred_element_type=F32)
-            if keep is not None:
-                keep[r] = acc
-            out[mine + r] = acc.astype(BF16)
+    def iterate(h, buf, out):
+        row = core * 64 + pf * 16
+
+        def body(s, carry):
+            anchors = (node + (s - ps) * ss) * 4
+            for r in range(4):
+                acc = sums[h][s * 4 + r]
+                for k in range(0, KA, 2):
+                    left = jnp.concatenate([buf[place(near[k + i, anchors + r])] for i in range(2)], axis=1)
+                    right = jnp.concatenate([row_tiles[s, r, k + i] for i in range(2)], axis=1)
+                    acc = acc + lax.dot_general(left, right, (((1,), (1,)), ((), ())), preferred_element_type=F32)
+                values[h][s * 4 + r] = acc
+                out[row + s * 4 + r] = acc.astype(BF16)
+            return carry
+
+        lax.fori_loop(0, 4, body, 0)
 
     def pipeline(h):
         yield from reduce_scatter(h)
-        mine = core * 64 + pf * 16 + ps * 4
-        for r in range(4):
-            shared[0][h][mine + r] = sums[h][r].astype(BF16)
+        row = core * 64 + pf * 16
+        add_blocks(4, shared[0][h], row + ps * 4, (sums[h], ps * 4))
+        yield from all_gather(h, shared[0][h], False)
+        for by, _ in ring:
+            at = turn(ps, by) * 4
+            add_blocks(4, sums[h], at, (shared[0][h], row + at))
+        if h == 0:
+            for copy in tile_sends:
+                copy.wait_recv()
+            own_tiles_copy.wait()
         for t in range(ITERS):
-            yield from all_gather(h, shared[t][h])
-            iterate(h, shared[t][h], shared[t + 1][h], values[h] if t == ITERS - 1 else None)
-        yield from all_gather(h, shared[ITERS][h])
+            iterate(h, shared[t][h], shared[t + 1][h])
+            yield from all_gather(h, shared[t + 1][h], True)
 
     lines = [pipeline(h) for h in range(H)]
     live = list(range(H))
@@ -300,7 +314,7 @@
                 live.remove(h)
 
     for r in range(4):
-        whole = jnp.concatenate([values[h][r] for h in range(H)], axis=0)
+        whole = jnp.concatenate([values[h][ps * 4 + r] for h in range(H)], axis=0)
         score_out[r * B : (r + 1) * B, :] = whole.T
 
     seeded_copy.wait()
@@ -326,7 +340,7 @@
         lax.fori_loop(0, PER // 2, body, 0)
         copy = pltpu.make_async_copy(
             ranked.at[pl.ds(c * PER * B, PER * B)], rank_out.at[pl.ds(c * PER * B, PER * B)],
-            local_sems.at[H + 1 + CHUNKS + c],
+            local_sems.at[H + 2 + CHUNKS + c],
         )
         copy.start()
         outs.append(copy)
@@ -341,7 +355,7 @@
                 for k in range(0, KN, 2):
                     pieces = []
                     for j in range(2):
-                        at = places[b * KN + k + j]
+                        at = place(lists[k + j, b])
                         pieces.append(jnp.concatenate([final[h][at] for h in range(H)], axis=0))
                     left = jnp.concatenate(pieces, axis=1)
                     right = jnp.concatenate([tiles[b, k + j] for j in range(2)], axis=1)
@@ -377,7 +391,7 @@
         copy.wait()
 
 
-def rest(places, near, held, seeded, atiles, tiles):
+def rest(lists, near, held, seeded, atiles, tiles):
     vm = lambda *shape, dtype=BF16: pltpu.VMEM(shape, dtype)
     per_half = lambda n, dtype=BF16: [pltpu.VMEM((n, R, B), dtype) for _ in range(H)]
     scratch = [
@@ -388,14 +402,16 @@
         vm(3, NB, B, dtype=F32),
         vm(NB * B, B),
     ]
-    for n in (64, 64, 16, 16, 16, 8, 8, 16, 16, 4, 4, 4, 2, 2, 4, 4):
+    for n in (64, 64, 16, 16, 16, 8, 8, 16, 16, 16):
         scratch += per_half(n)
-    scratch += per_half(4, F32) + per_half(4, F32)
+    scratch += [vm(4, 4, R, B) for _ in range(H)]
+    scratch += per_half(16, F32) + per_half(16, F32)
+    scratch += [vm(4, 4, KA, B, B)]
     for _ in range(ITERS + 1):
         scratch += per_half(NA)
     sems = pltpu.SemaphoreType.DMA
     scratch += [
-        sems((H * HALF_SEMS,)), sems((H * HALF_SEMS,)), sems((H + 1 + 2 * CHUNKS,)),
+        sems((H * HALF_SEMS + TILE_SEMS,)), sems((H * HALF_SEMS + TILE_SEMS,)), sems((H + 2 + 2 * CHUNKS,)),
         sems((3 * CHUNKS,)), sems((3 * CHUNKS,)),
     ]
     smem = pl.BlockSpec(memory_space=pltpu.SMEM)
@@ -403,24 +419,22 @@
     hbm = pl.BlockSpec(memory_space=pl.ANY)
     return pl.pallas_call(
         rest_kernel,
-        in_specs=[smem, smem, hbm, hbm, vmem, hbm],
+        in_specs=[smem, smem, hbm, hbm, hbm, hbm],
         out_specs=[hbm, vmem],
         out_shape=[jax.ShapeDtypeStruct((NB * B, B), BF16), jax.ShapeDtypeStruct((4 * B, B), F32)],
         scratch_shapes=scratch,
         compiler_params=pltpu.CompilerParams(
-            collective_id=0, has_side_effects=True, vmem_limit_bytes=58 << 20
+            collective_id=0, has_side_effects=True, vmem_limit_bytes=REST_VMEM << 20
         ),
         cost_estimate=pl.CostEstimate(flops=2 * NB * KN * B**3, bytes_accessed=28 << 20, transcendentals=0),
         name="rest",
-    )(places, near, held, seeded, atiles, tiles)
+    )(lists, near, held, seeded, atiles, tiles)
 
 
 def shards(node_scores, seeds, node_lists, node_tiles, anchor_lists, anchor_tiles):
-    places = place(node_lists).reshape(-1)
-    own_lists = lax.dynamic_slice_in_dim(anchor_lists, lax.axis_index("node") * 4, 4, 0)
-    near = place(own_lists).reshape(-1)
-    held, seeded = forward(places, seeds.reshape(1, B), node_scores, node_tiles)
-    ranking, anchor_scores = rest(places, near, held, seeded, anchor_tiles, node_tiles)
+    lists = node_lists.T
+    held, seeded = forward(lists, seeds.reshape(1, B), node_scores, node_tiles)
+    ranking, anchor_scores = rest(lists, anchor_lists.T, held, seeded, anchor_tiles, node_tiles)
     return (ranking, anchor_scores)
 
 

time: 128 us -> 111 us (0.87)
  local copies, waits for them, and re-layouts: 10.2 us -> 2.04 us
  Pallas kernels: 114 us -> 107 us
  other arithmetic: 1.49 us -> 0 us
    pallas_call x1, Pallas kernels: 102 us -> 91.2 us  [rest(): pl.pallas_call(rest_kernel, in_specs=[smem, smem, hbm, hbm, hbm, hbm], ou...]
    unnamed x14 -> x8, local copies, waits for them, and re-layouts: 9.29 us -> 2.04 us
    pallas_call x1, Pallas kernels: 12.7 us -> 16.2 us  [forward(): pl.pallas_call(forward_kernel, grid_spec=pltpu.PrefetchScalarGridSpec(num...]
    add x2 -> x0, other arithmetic: 1.49 us -> none  [place(): return core * 64 + first * 16 + second * 4 + slot]
where the time goes in v2:
time: 111 us; the launch traced here: 110 us
  Pallas kernels  107 us (96%)
  local copies, waits for them, and re-layouts  2.04 us (2%)
    pallas_call x1, Pallas kernels, rest(): pl.pallas_call(rest_kernel, in_specs=[smem, smem, hbm, hbm, hbm, hbm], ou...  91.2 us
    pallas_call x1, Pallas kernels, forward(): pl.pallas_call(forward_kernel, grid_spec=pltpu.PrefetchScalarGridSpec(num...  16.2 us

profile of v2, /device:TPU:0, one launch (start us, length us, event | category | flops | bytes accessed | tf_op | source)
XLA Modules:
  0.0 110.2 jit_solution(182375190036379248)
XLA Ops:
  0.6 0.0 copy-start
  0.6 0.0 copy-start.1
  0.7 0.0 copy-start.2
  0.7 16.2 %forward.1 = (bf16[2,128,64,128]{3,2,1,0:T(8,128)(2,1)}, bf16[64,128,128]{2,1,0:T(8,128)(2,1)}) custom-call(s32[8,64]{1,0:T(8,128)} %bitcast.3, s32[1,128]{1,0:T(1,128)} %bitcast.6, bf16[8192,128]{1,0:T(8,128)(2,1)} %scores.1, bf16[64,8,128,128]{3,2,1,0:T(8,128)(2,1)} %tiles_in.1), custom_call_target="tpu_custom_call" | custom-call | flops 2147483648 | bytes 25165824 | tf_op jit(solution)/shard_map/forward/pallas_call | solution.py:71
  16.9 0.0 copy-done
  16.9 0.0 copy-done.1
  16.9 0.0 copy-done.2
  16.9 91.2 %rest.1 = (bf16[8192,128]{1,0:T(8,128)(2,1)S(1)}, f32[512,128]{1,0:T(8,128)S(1)}) custom-call(s32[8,64]{1,0:T(8,128)S(1)} %bitcast.4, s32[4,128]{1,0:T(4,128)S(1)} %bitcast.5, bf16[2,128,64,128]{3,2,1,0:T(8,128)(2,1)} %get-tuple-element.4.held, bf16[64,128,128]{2,1,0:T(8,128)(2,1)} %get-tuple-element.5.seeded_in, bf16[4,4,128,128]{3,2,1,0:T(8,128)(2,1)S(1)} %copy-done, ...), custom_call_target="tpu_custom_call" | custom-call | flops 2147483648 | bytes 29360128 | tf_op jit(solution)/shard_map/rest/pallas_call | solution.py:420
  108.2 1.3 %copy.10 = bf16[8192,128]{1,0:T(8,128)(2,1)} copy(bf16[8192,128]{1,0:T(8,128)(2,1)S(1)} %get-tuple-element.8) | data formatting | bytes 4194304
  109.5 0.7 copy.11
Async XLA Ops:
  0.6 16.3 %copy-start = (bf16[4,4,128,128]{3,2,1,0:T(8,128)(2,1)S(1)}, bf16[4,4,128,128]{3,2,1,0:T(8,128)(2,1)}, u32[]{:S(2)}) copy-start(bf16[4,4,128,128]{3,2,1,0:T(8,128)(2,1)} %atiles.1) | copy-start | bytes 1572868
  0.6 16.3 %copy-start.1 = (s32[64,8]{0,1:T(8,128)S(1)}, s32[64,8]{0,1:T(8,128)}, u32[]{:S(2)}) copy-start(s32[64,8]{0,1:T(8,128)} %param.8) | copy-start | bytes 6148
  0.7 16.3 %copy-start.2 = (s32[128,4]{0,1:T(4,128)S(1)}, s32[128,4]{0,1:T(4,128)}, u32[]{:S(2)}) copy-start(s32[128,4]{0,1:T(4,128)} %param.10) | copy-start | bytes 6148

commit v3 on v2

--- a/solution.py
+++ b/solution.py
@@ -17,6 +17,7 @@
 NA = 128
 H = 2
 R = B // H
+PIECES = 4
 STEP = 8
 FORWARD_VMEM, REST_VMEM = 56, 50
 F32 = jnp.float32
@@ -31,62 +32,90 @@
     return (core << 6) + (first << 4) + (second << 2) + slot
 
 
-def forward_kernel(lists, seeds, scores, tiles, held, seeded, total):
-    step = pl.program_id(0)
+def forward_kernel(
+    lists, seeds, scores_in, tiles_in, held, seeded_out,
+    total, narrow, tiles, scores, seeded, out_sems, tile_sems, score_sems, seeded_sems,
+):
     start_row = lax.axis_index("node") * (NB * B)
-
-    @pl.when(step == 0)
-    def _():
-        def clear(i, carry):
-            total[i] = jnp.zeros((B, B), F32)
+    rows_of = lambda g: pl.ds(pl.multiple_of(g * (STEP * B), STEP * B), STEP * B)
+    blocks_of = lambda g: pl.ds(g * STEP, STEP)
+    score_copy = lambda g: pltpu.make_async_copy(scores_in.at[rows_of(g)], scores.at[rows_of(g)], score_sems.at[g])
+    tile_copy = lambda g: pltpu.make_async_copy(tiles_in.at[blocks_of(g)], tiles.at[blocks_of(g)], tile_sems.at[g])
+    seeded_copy = lambda g: pltpu.make_async_copy(seeded.at[blocks_of(g)], seeded_out.at[blocks_of(g)], seeded_sems.at[g])
+    for g in range(NB // STEP):
+        score_copy(g).start()
+        tile_copy(g).start()
+
+    def clear(i, carry):
+        for u in range(4):
+            total[i * 4 + u] = jnp.zeros((B, B), F32)
+        return carry
+
+    lax.fori_loop(0, NA // 4, clear, 0)
+    wanted = seeds[...]
+
+    def group(g, carry):
+        score_copy(g).wait()
+        tile_copy(g).wait()
+        for u in range(STEP):
+            b = g * STEP + u
+            at_rows = pl.ds(pl.multiple_of(b * B, B), B)
+            rows = lax.broadcasted_iota(jnp.int32, (B, B), 0) + (start_row + b * B)
+            hit = (rows == wanted).astype(F32)
+            block = scores[at_rows, :].astype(F32) + SEED_GAIN * hit
+            flipped = block.astype(BF16).T
+            seeded[b] = flipped
+            for k in range(KN):
+                term = jnp.dot(flipped, tiles[b, k], preferred_element_type=F32)
+                total[place(lists[k, b])] += term
+        seeded_copy(g).start()
+        return carry
+
+    lax.fori_loop(0, NB // STEP, group, 0)
+    copies = []
+    for c in range(PIECES):
+
+        def body(i, carry):
+            for u in range(4):
+                a = c * (NA // PIECES) + i * 4 + u
+                whole = total[a].astype(BF16)
+                for h in range(H):
+                    narrow[h, a] = whole[h * R : (h + 1) * R]
             return carry
 
-        lax.fori_loop(0, NA, clear, 0, unroll=4)
-
-    wanted = seeds[...]
-    for b in range(STEP):
-        first = start_row + (step * STEP + b) * B
-        rows = lax.broadcasted_iota(jnp.int32, (B, B), 0) + first
-        hit = (rows == wanted).astype(F32)
-        block = scores[b * B : (b + 1) * B, :].astype(F32) + SEED_GAIN * hit
-        flipped = block.T.astype(BF16)
-        seeded[b] = flipped
-        for k in range(KN):
-            term = jnp.dot(flipped, tiles[b, k], preferred_element_type=F32)
-            at = place(lists[k, step * STEP + b])
-            total[at] += term
-
-    @pl.when(step == pl.num_programs(0) - 1)
-    def _():
-        def narrow(i, carry):
-            whole = total[i].astype(BF16)
-            for h in range(H):
-                held[h, i] = whole[h * R : (h + 1) * R]
-            return carry
-
-        lax.fori_loop(0, NA, narrow, 0, unroll=4)
+        lax.fori_loop(0, NA // PIECES // 4, body, 0)
+        at = pl.ds(c * (NA // PIECES), NA // PIECES)
+        for h in range(H):
+            copy = pltpu.make_async_copy(narrow.at[h, at], held.at[h, at], out_sems.at[c * H + h])
+            copy.start()
+            copies.append(copy)
+    for copy in copies:
+        copy.wait()
+    for g in range(NB // STEP):
+        seeded_copy(g).wait()
 
 
 def forward(lists, seeds, scores, tiles):
+    hbm = pl.BlockSpec(memory_space=pl.ANY)
+    sems = pltpu.SemaphoreType.DMA
     return pl.pallas_call(
         forward_kernel,
-        grid_spec=pltpu.PrefetchScalarGridSpec(
-            num_scalar_prefetch=1,
-            grid=(NB // STEP,),
-            in_specs=[
-                pl.BlockSpec((1, B), lambda g, p: (0, 0)),
-                pl.BlockSpec((STEP * B, B), lambda g, p: (g, 0)),
-                pl.BlockSpec((STEP, KN, B, B), lambda g, p: (g, 0, 0, 0)),
-            ],
-            out_specs=[
-                pl.BlockSpec((H, NA, R, B), lambda g, p: (0, 0, 0, 0)),
-                pl.BlockSpec((STEP, B, B), lambda g, p: (g, 0, 0)),
-            ],
-            scratch_shapes=[pltpu.VMEM((NA, B, B), F32)],
-        ),
+        in_specs=[pl.BlockSpec(memory_space=pltpu.SMEM), pl.BlockSpec(memory_space=pltpu.VMEM), hbm, hbm],
+        out_specs=[hbm, hbm],
         out_shape=[
             jax.ShapeDtypeStruct((H, NA, R, B), BF16),
             jax.ShapeDtypeStruct((NB, B, B), BF16),
+        ],
+        scratch_shapes=[
+            pltpu.VMEM((NA, B, B), F32),
+            pltpu.VMEM((H, NA, R, B), BF16),
+            pltpu.VMEM((NB, KN, B, B), BF16),
+            pltpu.VMEM((NB * B, B), BF16),
+            pltpu.VMEM((NB, B, B), BF16),
+            sems((PIECES * H,)),
+            sems((NB // STEP,)),
+            sems((NB // STEP,)),
+            sems((NB // STEP,)),
         ],
         compiler_params=pltpu.CompilerParams(vmem_limit_bytes=FORWARD_VMEM << 20),
         cost_estimate=pl.CostEstimate(flops=2 * NB * KN * B**3, bytes_accessed=24 << 20, transcendentals=0),
@@ -96,6 +125,7 @@
 
 CHUNKS = 4
 PER = NB // CHUNKS
+UNROLL = 8
 RS_SEMS = 4 + 6 + 3
 AG_SEMS = 3 + 6 + 4
 HALF_SEMS = RS_SEMS + (ITERS + 1) * AG_SEMS
@@ -105,7 +135,7 @@
 def rest_kernel(lists, near, held, seeded_in, atiles, tiles_in, rank_out, score_out, *scratch):
     scratch = list(scratch)
     take = lambda n: [scratch.pop(0) for _ in range(n)]
-    tiles, seeded, resid, energy, others, ranked = take(6)
+    tiles, seeded, resid, energy, others = take(5)
     own, mate = take(H), take(H)
     far, up, down, ra, rb, gm, gp = (take(H) for _ in range(7))
     out2, in2 = take(H), take(H)
@@ -138,7 +168,9 @@
     own_copies = [local(held.at[h, pl.ds(core * 64, 64)], own[h]) for h in range(H)]
     own_tiles_copy = local(atiles, row_tiles.at[ps])
     seeded_copy = local(seeded_in, seeded)
-    tile_copies = [local(tiles_in.at[pl.ds(i * PER, PER)], tiles.at[pl.ds(i * PER, PER)]) for i in range(CHUNKS)]
+    load_tiles = lambda: [
+        local(tiles_in.at[pl.ds(i * PER, PER)], tiles.at[pl.ds(i * PER, PER)]) for i in range(CHUNKS)
+    ]
 
     barrier = pltpu.get_barrier_semaphore()
     for peer in (sib, f_up, f_dn, s_up, s_dn, s_far):
@@ -155,32 +187,31 @@
         count[h] += 1
         copy = pltpu.make_async_remote_copy(
             src_ref=src, dst_ref=dst, send_sem=send_sems.at[i], recv_sem=recv_sems.at[i],
-            device_id={"node": peer}, device_id_type=MESH,
+            device_id=peer if isinstance(peer, dict) else {"node": peer}, device_id_type=MESH,
         )
         copy.start()
         started.append(copy)
         return copy
 
-    tile_sends = []
-
-    def share_tiles(n):
-        for _ in range(n):
-            i = len(tile_sends)
-            if i < 12:
-                r, (_, peer) = i // 3, ring[i % 3]
-                tile_sends.append(send(H, atiles.at[r], row_tiles.at[ps, r], peer))
+    def pass_tiles_on():
+        for copy in tile_hops:
+            copy.wait_recv()
+        return [
+            send(H, row_tiles.at[turn(ps, by), pb], row_tiles.at[turn(ps, by), pb], {"pb": turn(pb, d)})
+            for by, _ in ring for d in (1, 2, 3)
+        ]
 
     def add_blocks(n, dst, dst_at, *terms):
         def body(i, carry):
-            for u in range(2):
-                j = i * 2 + u
+            for u in range(4):
+                j = i * 4 + u
                 acc = terms[0][0][terms[0][1] + j].astype(F32)
                 for ref, at in terms[1:]:
                     acc = acc + ref[at + j].astype(F32)
                 dst[dst_at + j] = acc.astype(dst.dtype)
             return carry
 
-        lax.fori_loop(0, n // 2, body, 0)
+        lax.fori_loop(0, n // 4, body, 0)
 
     def reduce_scatter(h):
         o, m = own[h], mate[h]
@@ -225,7 +256,6 @@
             to = turn(ps, by) * 4
             add_blocks(4, out2[h], to, *part(turn(ps, by), 0))
             hops.append(send(h, out2[h].at[pl.ds(to, 4)], in2[h].at[ps], peer))
-        share_tiles(3)
         yield
         add_blocks(4, sums[h], ps * 4, *part(ps, 0))
         for copy in hops:
@@ -241,7 +271,6 @@
         go = lambda start, n, peer: send(h, at(start, n), at(start, n), peer)
         if not whole:
             hops = [go(mine, 4, peer) for _, peer in ring]
-            share_tiles(3)
             yield
             for copy in hops:
                 copy.wait_recv()
@@ -294,7 +323,7 @@
             at = turn(ps, by) * 4
             add_blocks(4, sums[h], at, (shared[0][h], row + at))
         if h == 0:
-            for copy in tile_sends:
+            for copy in tile_passes:
                 copy.wait_recv()
             own_tiles_copy.wait()
         for t in range(ITERS):
@@ -303,9 +332,13 @@
 
     lines = [pipeline(h) for h in range(H)]
     live = list(range(H))
-    next(lines[0])
-    if H > 1:
-        next(lines[1])
+    for line in lines:
+        next(line)
+    tile_hops = [send(H, atiles.at[pb], row_tiles.at[ps, pb], peer) for _, peer in ring]
+    for line in lines:
+        next(line)
+    tile_passes = pass_tiles_on()
+    tile_copies = load_tiles()
     while live:
         for h in list(live):
             try:
@@ -320,37 +353,30 @@
     seeded_copy.wait()
     final = shared[ITERS]
     esends = []
-    outs = []
 
     def finish(c):
         for copy in esends[c]:
             copy.wait_recv()
 
         def body(i, carry):
-            for u in range(2):
-                b = c * PER + i * 2 + u
+            for u in range(UNROLL):
+                b = c * PER + i * UNROLL + u
                 tot = energy[pl.ds(b, 1), :]
                 for d in range(3):
                     tot = tot + others[d, pl.ds(b, 1), :]
                 scale = lax.rsqrt(tot / 512.0 + EPS)
                 block = (resid[b] * scale).astype(BF16)
-                ranked[pl.ds(pl.multiple_of(b * B, B), B), :] = block.T
+                rank_out[pl.ds(pl.multiple_of(b * B, B), B), :] = block.T
             return carry
 
-        lax.fori_loop(0, PER // 2, body, 0)
-        copy = pltpu.make_async_copy(
-            ranked.at[pl.ds(c * PER * B, PER * B)], rank_out.at[pl.ds(c * PER * B, PER * B)],
-            local_sems.at[H + 2 + CHUNKS + c],
-        )
-        copy.start()
-        outs.append(copy)
+        lax.fori_loop(0, PER // UNROLL, body, 0)
 
     for c in range(CHUNKS):
         tile_copies[c].wait()
 
         def body(i, carry):
-            for u in range(4):
-                b = c * PER + i * 4 + u
+            for u in range(UNROLL):
+                b = c * PER + i * UNROLL + u
                 acc = None
                 for k in range(0, KN, 2):
                     pieces = []
@@ -366,7 +392,7 @@
                 energy[pl.ds(b, 1), :] = jnp.sum(res * res, axis=0, keepdims=True)
             return carry
 
-        lax.fori_loop(0, PER // 4, body, 0)
+        lax.fori_loop(0, PER // UNROLL, body, 0)
         group = []
         for d in (1, 2, 3):
             i = c * 3 + d - 1
@@ -378,17 +404,14 @@
             copy.start()
             group.append(copy)
         esends.append(group)
-        if c > 0:
-            finish(c - 1)
-    finish(CHUNKS - 1)
+    for c in range(CHUNKS):
+        finish(c)
 
     for copy in started:
         copy.wait_send()
     for group in esends:
         for copy in group:
             copy.wait_send()
-    for copy in outs:
-        copy.wait()
 
 
 def rest(lists, near, held, seeded, atiles, tiles):
@@ -400,7 +423,6 @@
         vm(NB, B, B, dtype=F32),
         vm(NB, B, dtype=F32),
         vm(3, NB, B, dtype=F32),
-        vm(NB * B, B),
     ]
     for n in (64, 64, 16, 16, 16, 8, 8, 16, 16, 16):
         scratch += per_half(n)
@@ -411,7 +433,7 @@
         scratch += per_half(NA)
     sems = pltpu.SemaphoreType.DMA
     scratch += [
-        sems((H * HALF_SEMS + TILE_SEMS,)), sems((H * HALF_SEMS + TILE_SEMS,)), sems((H + 2 + 2 * CHUNKS,)),
+        sems((H * HALF_SEMS + TILE_SEMS,)), sems((H * HALF_SEMS + TILE_SEMS,)), sems((H + 2 + CHUNKS,)),
         sems((3 * CHUNKS,)), sems((3 * CHUNKS,)),
     ]
     smem = pl.BlockSpec(memory_space=pltpu.SMEM)
@@ -420,7 +442,7 @@
     return pl.pallas_call(
         rest_kernel,
         in_specs=[smem, smem, hbm, hbm, hbm, hbm],
-        out_specs=[hbm, vmem],
+        out_specs=[vmem, vmem],
         out_shape=[jax.ShapeDtypeStruct((NB * B, B), BF16), jax.ShapeDtypeStruct((4 * B, B), F32)],
         scratch_shapes=scratch,
         compiler_params=pltpu.CompilerParams(

time: 111 us -> 94.5 us (0.85)
  Pallas kernels: 107 us -> 90.4 us
    pallas_call x1, Pallas kernels: 91.2 us -> 78.9 us  [rest(): pl.pallas_call(rest_kernel, in_specs=[smem, smem, hbm, hbm, hbm, hbm], ou...]
    pallas_call x1, Pallas kernels: 16.2 us -> 11.5 us  [forward(): pl.pallas_call(forward_kernel, in_specs=[pl.BlockSpec(memory_space=pltpu....]
where the time goes in v3:
time: 94.5 us; the launch traced here: 93.1 us
  Pallas kernels  90.4 us (96%)
  local copies, waits for them, and re-layouts  2.04 us (2%)
    pallas_call x1, Pallas kernels, rest(): pl.pallas_call(rest_kernel, in_specs=[smem, smem, hbm, hbm, hbm, hbm], ou...  78.9 us
    pallas_call x1, Pallas kernels, forward(): pl.pallas_call(forward_kernel, in_specs=[pl.BlockSpec(memory_space=pltpu....  11.5 us
    unnamed x8, local copies, waits for them, and re-layouts  2.04 us

profile of v3, /device:TPU:0, one launch (start us, length us, event | category | flops | bytes accessed | tf_op | source)
XLA Modules:
  0.0 93.1 jit_solution(17738768089350869854)
XLA Ops:
  0.6 0.0 copy-start
  0.6 0.0 copy-start.1
  0.7 0.0 copy-start.2
  0.7 11.5 %forward.1 = (bf16[2,128,64,128]{3,2,1,0:T(8,128)(2,1)}, bf16[64,128,128]{2,1,0:T(8,128)(2,1)}) custom-call(s32[8,64]{1,0:T(8,128)} %bitcast.3, s32[1,128]{1,0:T(1,128)} %bitcast.6, bf16[8192,128]{1,0:T(8,128)(2,1)} %scores_in.1, bf16[64,8,128,128]{3,2,1,0:T(8,128)(2,1)} %tiles_in.3), custom_call_target="tpu_custom_call" | custom-call | flops 2147483648 | bytes 25165824 | tf_op jit(solution)/shard_map/forward/pallas_call | solution.py:101
  12.2 0.0 copy-done
  12.2 0.0 copy-done.1
  12.2 0.0 copy-done.2
  12.2 78.9 %rest.1 = (bf16[8192,128]{1,0:T(8,128)(2,1)S(1)}, f32[512,128]{1,0:T(8,128)S(1)}) custom-call(s32[8,64]{1,0:T(8,128)S(1)} %bitcast.4, s32[4,128]{1,0:T(4,128)S(1)} %bitcast.5, bf16[2,128,64,128]{3,2,1,0:T(8,128)(2,1)} %get-tuple-element.4.held, bf16[64,128,128]{2,1,0:T(8,128)(2,1)} %get-tuple-element.5.seeded_in, bf16[4,4,128,128]{3,2,1,0:T(8,128)(2,1)S(1)} %copy-done, ...), custom_call_target="tpu_custom_call" | custom-call | flops 2147483648 | bytes 29360128 | tf_op jit(solution)/shard_map/rest/pallas_call | solution.py:442
  91.1 1.3 %copy.10 = bf16[8192,128]{1,0:T(8,128)(2,1)} copy(bf16[8192,128]{1,0:T(8,128)(2,1)S(1)} %get-tuple-element.8) | data formatting | bytes 4194304
  92.4 0.7 copy.11
Async XLA Ops:
  0.6 11.5 %copy-start = (bf16[4,4,128,128]{3,2,1,0:T(8,128)(2,1)S(1)}, bf16[4,4,128,128]{3,2,1,0:T(8,128)(2,1)}, u32[]{:S(2)}) copy-start(bf16[4,4,128,128]{3,2,1,0:T(8,128)(2,1)} %atiles.1) | copy-start | bytes 1572868
  0.6 11.5 %copy-start.1 = (s32[64,8]{0,1:T(8,128)S(1)}, s32[64,8]{0,1:T(8,128)}, u32[]{:S(2)}) copy-start(s32[64,8]{0,1:T(8,128)} %param.8) | copy-start | bytes 6148
  0.7 11.5 %copy-start.2 = (s32[128,4]{0,1:T(4,128)S(1)}, s32[128,4]{0,1:T(4,128)}, u32[]{:S(2)}) copy-start(s32[128,4]{0,1:T(4,128)} %param.10) | copy-start | bytes 6148

commit v4 on v3

--- a/solution.py
+++ b/solution.py
@@ -18,7 +18,7 @@
 H = 2
 R = B // H
 PIECES = 4
-STEP = 8
+STEP = 16
 FORWARD_VMEM, REST_VMEM = 56, 50
 F32 = jnp.float32
 BF16 = jnp.bfloat16
@@ -125,7 +125,7 @@
 
 CHUNKS = 4
 PER = NB // CHUNKS
-UNROLL = 8
+UNROLL = 16
 RS_SEMS = 4 + 6 + 3
 AG_SEMS = 3 + 6 + 4
 HALF_SEMS = RS_SEMS + (ITERS + 1) * AG_SEMS
@@ -293,7 +293,6 @@
         ua2.wait_recv()
         db2.wait_recv()
         across.append(go(far_, 16, sib))
-        yield
         for copy in across:
             copy.wait_recv()
 

time: 94.5 us -> 93.2 us (0.986)
  no operation moved by 1% of the time
where the time goes in v4:
time: 93.2 us; the launch traced here: 92.6 us
  Pallas kernels  89.9 us (96%)
  local copies, waits for them, and re-layouts  2.04 us (2%)
    pallas_call x1, Pallas kernels, rest(): pl.pallas_call(rest_kernel, in_specs=[smem, smem, hbm, hbm, hbm, hbm], ou...  78.4 us
    pallas_call x1, Pallas kernels, forward(): pl.pallas_call(forward_kernel, in_specs=[pl.BlockSpec(memory_space=pltpu....  11.4 us
    unnamed x8, local copies, waits for them, and re-layouts  2.04 us

profile of v4, /device:TPU:0, one launch (start us, length us, event | category | flops | bytes accessed | tf_op | source)
XLA Modules:
  0.0 92.6 jit_solution(8662526668600602684)
XLA Ops:
  0.6 0.0 copy-start
  0.6 0.0 copy-start.1
  0.7 0.0 copy-start.2
  0.7 11.4 %forward.1 = (bf16[2,128,64,128]{3,2,1,0:T(8,128)(2,1)}, bf16[64,128,128]{2,1,0:T(8,128)(2,1)}) custom-call(s32[8,64]{1,0:T(8,128)} %bitcast.3, s32[1,128]{1,0:T(1,128)} %bitcast.6, bf16[8192,128]{1,0:T(8,128)(2,1)} %scores_in.1, bf16[64,8,128,128]{3,2,1,0:T(8,128)(2,1)} %tiles_in.3), custom_call_target="tpu_custom_call" | custom-call | flops 2147483648 | bytes 25165824 | tf_op jit(solution)/shard_map/forward/pallas_call | solution.py:101
  12.1 0.0 copy-done
  12.1 0.0 copy-done.1
  12.1 0.0 copy-done.2
  12.1 78.4 %rest.1 = (bf16[8192,128]{1,0:T(8,128)(2,1)S(1)}, f32[512,128]{1,0:T(8,128)S(1)}) custom-call(s32[8,64]{1,0:T(8,128)S(1)} %bitcast.4, s32[4,128]{1,0:T(4,128)S(1)} %bitcast.5, bf16[2,128,64,128]{3,2,1,0:T(8,128)(2,1)} %get-tuple-element.4.held, bf16[64,128,128]{2,1,0:T(8,128)(2,1)} %get-tuple-element.5.seeded_in, bf16[4,4,128,128]{3,2,1,0:T(8,128)(2,1)S(1)} %copy-done, ...), custom_call_target="tpu_custom_call" | custom-call | flops 2147483648 | bytes 29360128 | tf_op jit(solution)/shard_map/rest/pallas_call | solution.py:441
  90.6 1.3 %copy.10 = bf16[8192,128]{1,0:T(8,128)(2,1)} copy(bf16[8192,128]{1,0:T(8,128)(2,1)S(1)} %get-tuple-element.8) | data formatting | bytes 4194304
  91.9 0.7 copy.11
Async XLA Ops:
  0.6 11.5 %copy-start = (bf16[4,4,128,128]{3,2,1,0:T(8,128)(2,1)S(1)}, bf16[4,4,128,128]{3,2,1,0:T(8,128)(2,1)}, u32[]{:S(2)}) copy-start(bf16[4,4,128,128]{3,2,1,0:T(8,128)(2,1)} %atiles.1) | copy-start | bytes 1572868
  0.6 11.5 %copy-start.1 = (s32[64,8]{0,1:T(8,128)S(1)}, s32[64,8]{0,1:T(8,128)}, u32[]{:S(2)}) copy-start(s32[64,8]{0,1:T(8,128)} %param.8) | copy-start | bytes 6148
  0.7 11.5 %copy-start.2 = (s32[128,4]{0,1:T(4,128)S(1)}, s32[128,4]{0,1:T(4,128)}, u32[]{:S(2)}) copy-start(s32[128,4]{0,1:T(4,128)} %param.10) | copy-start | bytes 6148

commit v5 on v4

--- a/solution.py
+++ b/solution.py
@@ -227,6 +227,7 @@
         add_blocks(16, far[h], 0, (o, at), (m, at))
         a1 = send(h, far[h].at[pl.ds(0, 8)], ra[h], f_up)
         b1 = send(h, far[h].at[pl.ds(8, 8)], rb[h], f_dn)
+        yield
         at_up, at_dn = turn(pf, 1) * 16, turn(pf, -1) * 16
         got[1].wait_recv()
         add_blocks(8, up[h], 8, (o, at_up + 8), (m, at_up + 8))
@@ -331,11 +332,13 @@
 
     lines = [pipeline(h) for h in range(H)]
     live = list(range(H))
-    for line in lines:
-        next(line)
+    for turn_no in range(1):
+        for line in lines:
+            next(line)
     tile_hops = [send(H, atiles.at[pb], row_tiles.at[ps, pb], peer) for _, peer in ring]
-    for line in lines:
-        next(line)
+    for turn_no in range(3):
+        for line in lines:
+            next(line)
     tile_passes = pass_tiles_on()
     tile_copies = load_tiles()
     while live:

time: 93.2 us -> 93 us (level)
  no operation moved by 1% of the time
where the time goes in v5:
time: 93 us; the launch traced here: 92.4 us
  Pallas kernels  89.7 us (96%)
  local copies, waits for them, and re-layouts  2.04 us (2%)
    pallas_call x1, Pallas kernels, rest(): pl.pallas_call(rest_kernel, in_specs=[smem, smem, hbm, hbm, hbm, hbm], ou...  78.3 us
    pallas_call x1, Pallas kernels, forward(): pl.pallas_call(forward_kernel, in_specs=[pl.BlockSpec(memory_space=pltpu....  11.4 us
    unnamed x8, local copies, waits for them, and re-layouts  2.04 us

profile of v5, /device:TPU:0, one launch (start us, length us, event | category | flops | bytes accessed | tf_op | source)
XLA Modules:
  0.0 92.4 jit_solution(7669482021333727049)
XLA Ops:
  0.6 0.0 copy-start
  0.6 0.0 copy-start.1
  0.7 0.0 copy-start.2
  0.7 11.4 %forward.1 = (bf16[2,128,64,128]{3,2,1,0:T(8,128)(2,1)}, bf16[64,128,128]{2,1,0:T(8,128)(2,1)}) custom-call(s32[8,64]{1,0:T(8,128)} %bitcast.3, s32[1,128]{1,0:T(1,128)} %bitcast.6, bf16[8192,128]{1,0:T(8,128)(2,1)} %scores_in.1, bf16[64,8,128,128]{3,2,1,0:T(8,128)(2,1)} %tiles_in.3), custom_call_target="tpu_custom_call" | custom-call | flops 2147483648 | bytes 25165824 | tf_op jit(solution)/shard_map/forward/pallas_call | solution.py:101
  12.1 0.0 copy-done
  12.1 0.0 copy-done.1
  12.1 0.0 copy-done.2
  12.1 78.3 %rest.1 = (bf16[8192,128]{1,0:T(8,128)(2,1)S(1)}, f32[512,128]{1,0:T(8,128)S(1)}) custom-call(s32[8,64]{1,0:T(8,128)S(1)} %bitcast.4, s32[4,128]{1,0:T(4,128)S(1)} %bitcast.5, bf16[2,128,64,128]{3,2,1,0:T(8,128)(2,1)} %get-tuple-element.4.held, bf16[64,128,128]{2,1,0:T(8,128)(2,1)} %get-tuple-element.5.seeded_in, bf16[4,4,128,128]{3,2,1,0:T(8,128)(2,1)S(1)} %copy-done, ...), custom_call_target="tpu_custom_call" | custom-call | flops 2147483648 | bytes 29360128 | tf_op jit(solution)/shard_map/rest/pallas_call | solution.py:444
  90.4 1.3 %copy.10 = bf16[8192,128]{1,0:T(8,128)(2,1)} copy(bf16[8192,128]{1,0:T(8,128)(2,1)S(1)} %get-tuple-element.8) | data formatting | bytes 4194304
  91.7 0.7 copy.11
Async XLA Ops:
  0.6 11.5 %copy-start = (bf16[4,4,128,128]{3,2,1,0:T(8,128)(2,1)S(1)}, bf16[4,4,128,128]{3,2,1,0:T(8,128)(2,1)}, u32[]{:S(2)}) copy-start(bf16[4,4,128,128]{3,2,1,0:T(8,128)(2,1)} %atiles.1) | copy-start | bytes 1572868
  0.6 11.5 %copy-start.1 = (s32[64,8]{0,1:T(8,128)S(1)}, s32[64,8]{0,1:T(8,128)}, u32[]{:S(2)}) copy-start(s32[64,8]{0,1:T(8,128)} %param.8) | copy-start | bytes 6148
  0.7 11.5 %copy-start.2 = (s32[128,4]{0,1:T(4,128)S(1)}, s32[128,4]{0,1:T(4,128)}, u32[]{:S(2)}) copy-start(s32[128,4]{0,1:T(4,128)} %param.10) | copy-start | bytes 6148
